TPU v7x, 32 devices: a whole 2x2x4 slice. The times are simulated.
32 devices in a mesh: section: 16 (over z, x, core), tensor: 2 (over y).
Axes of the slice: x: 2, y: 2, z: 4, core: 2. Of those that a mesh axis runs over, the one named last changes fastest.
Arguments:
- section_rows: bfloat16 [3, 2048, 8192], P(None, 'section', 'tensor'), may hold values from -6 to 6
- student_rows: bfloat16 [3, 2048, 3584], P(None, 'section'), may hold values from -6 to 6
- proj: bfloat16 [3584, 8192], P('section', 'tensor'), may hold values from -0.09375 to 0.09375
- gains: float32 [3, 8192], P(None, 'tensor'), may hold values from 0.1 to 1.9
- offsets: int32 [16], replicated, may hold values from 0 to 15, each once
Outputs:
- loss: float32 [], replicated
- grad_student: float32 [3, 2048, 3584], P(None, 'section', 'tensor')
- grad_proj: float32 [3584, 8192], P('section', 'tensor')
- grad_gains: float32 [3, 8192], P(None, 'tensor')
Inputs may be any that keep to these rules, and one draw needn't show every extreme that they name: `offsets`: each shard is held by exactly one rank.
All inputs are finite; a program needn't handle non-finite values.
Results may differ from a plain program's by a relative error of at most 0.01.
Values may be sent and summed in bfloat16 or wider, within the bound.
A program may use at most 192 MiB of HBM per device.

v0:
```python
import jax
import jax.numpy as jnp
from jax import lax
from jax.sharding import PartitionSpec as P


def body(section_rows, student_rows, proj, gains, offsets):
    sections = lax.axis_size("section")
    tensors = lax.axis_size("tensor")
    seq_dev = student_rows.shape[1]
    width = section_rows.shape[2]
    student_width = student_rows.shape[2]
    per_source = seq_dev // sections
    total_rows = 3 * seq_dev * sections
    rescale = float(total_rows) ** (-0.5)
    blocks = section_rows.reshape(3, sections, per_source, 1, width)
    outgoing = jnp.take(blocks, offsets, axis=1)
    incoming = lax.all_to_all(outgoing, "section", split_axis=1, concat_axis=3, tiled=True)
    target = incoming.reshape(3, seq_dev, width).astype(jnp.float32)
    whole_proj = lax.all_gather(proj, "section", axis=0, tiled=True)
    flat_student = student_rows.reshape(3 * seq_dev, student_width)
    pred = jnp.dot(flat_student, whole_proj, preferred_element_type=jnp.float32).reshape(
        3, seq_dev, width
    )
    squares = jnp.sum(target * target, axis=-1)
    scale = lax.psum(squares, "tensor") / (width * tensors) + 1e-06
    diff = gains[:, None, :] * pred - target
    ratio = diff / scale[:, :, None]
    steer = (gains[:, None, :] * ratio).astype(jnp.bfloat16)
    flat_steer = steer.reshape(3 * seq_dev, width)
    partial_student = lax.dot_general(
        flat_steer, whole_proj, (((1,), (1,)), ((), ())), preferred_element_type=jnp.float32
    )
    grad_student = lax.psum_scatter(
        partial_student.reshape(3, seq_dev, student_width).astype(jnp.bfloat16),
        "tensor",
        scatter_dimension=2,
        tiled=True,
    ).astype(jnp.float32)
    grad_gains = lax.psum(jnp.sum(ratio * pred, axis=1), "section") * rescale
    loss = lax.psum(jnp.sum(diff * ratio), ("section", "tensor")) / (
        2.0 * total_rows * width * tensors
    )
    term = lax.dot_general(
        flat_student, flat_steer, (((0,), (0,)), ((), ())), preferred_element_type=jnp.float32
    )
    grad_proj = (
        lax.psum_scatter(
            term.astype(jnp.bfloat16), "section", scatter_dimension=0, tiled=True
        ).astype(jnp.float32)
        * rescale
    )
    return (loss, grad_student, grad_proj, grad_gains)


def solution(mesh):
    return jax.shard_map(
        body,
        mesh=mesh,
        in_specs=(
            P(None, "section", "tensor"),
            P(None, "section", None),
            P("section", "tensor"),
            P(None, "tensor"),
            P(),
        ),
        out_specs=(P(), P(None, "section", "tensor"), P("section", "tensor"), P(None, "tensor")),
        check_vma=False,
    )
```

profile of v0, /device:TPU:8, one launch (start us, length us, event | category | flops | bytes accessed | tf_op | source)
XLA Modules:
  0.0 631.1 jit_solution(887531318404848249)
XLA Ops:
  7.2 0.0 copy-start
  7.2 0.0 copy-start.4
  7.2 0.0 all-gather.2.cloned.1.call-start
  7.2 0.7 all-gather.2.cloned.1.call-update
  7.9 0.0 reduce-scatter.5.cloned.1.call-start
  8.0 0.8 compare_select_fusion
  8.8 0.3 copy-done
  9.1 2.4 gather_fusion
  11.5 0.0 copy-done.4
  11.5 2.3 fusion.10
  13.7 110.2 %all_to_all.4 = bf16[3,16,8,1,4096]{4,2,0,3,1:T(8,128)(2,1)S(1)} all-to-all(bf16[3,16,8,1,4096]{4,2,0,3,1:T(8,128)(2,1)S(1)} %fusion.10), channel_id=1, replica_groups=mesh['section'=16,'tensor'=2] {'section'}, dimensions={1} | all-to-all | bytes 6291456 | tf_op jit(solution)/shard_map/all_to_all | solution.py:18
  123.9 0.7 fusion.6
  124.6 0.1 copy.22
  124.7 0.1 reduce_sum.33
  124.8 0.8 convert_bitcast_fusion
  125.5 0.0 copy-start.2
  125.6 0.0 copy-start.3
  125.6 6.3 copy.20
  131.8 5.1 psum.21
  137.0 89.6 %all-gather.2.cloned.1.call-done = bf16[3584,4096]{1,0:T(8,128)(2,1)} async-done(((bf16[224,4096]{1,0:T(8,128)(2,1)}), bf16[3584,4096]{1,0:T(8,128)(2,1)}) %all-gather.2.cloned.1.call-update) | async-done | bytes 29360144 | tf_op jit(solution)/shard_map/all_gather | solution.py:20
  226.6 0.0 copy-done.2
  226.6 0.0 copy-done.3
  226.6 20.9 %multiply_reduce_fusion = (f32[3,4096]{1,0:T(4,128)S(1)}, f32[]{:T(128)}, f32[3,128,4096]{2,1,0:T(8,128)}) fusion(f32[3,128]{1,0:T(4,128)S(1)} %multiply_add_fusion, f32[3,128,4096]{2,1,0:T(8,128)} %bitcast.38, f32[3,4096]{1,0:T(4,128)S(1)} %copy-done.3, bf16[3,128,3584]{2,1,0:T(8,128)(2,1)S(1)} %copy-done.2, ...), kind=kOutput, calls=%fused_computation.11 | convolution fusion | flops 11285286912 | bytes 44795396 | tf_op jit(solution)/shard_map/dot_general | solution.py:22
  247.5 22.4 %fusion.7 = bf16[3,128,3584]{2,1,0:T(8,128)(2,1)} fusion(bf16[3584,4096]{1,0:T(8,128)(2,1)} %all-gather.2.cloned.1.call-done, f32[3,4096]{1,0:T(4,128)S(1)} %copy-done.3, f32[3,128]{1,0:T(4,128)S(1)} %multiply_add_fusion, f32[3,128,4096]{2,1,0:T(8,128)} %bitcast.39, f32[3,128,4096]{2,1,0:T(8,128)} %get-tuple-element.22), kind=kOutput, calls=%fused_computation.15 | convolution fusion | flops 11283529728 | bytes 44746240 | tf_op jit(solution)/shard_map/dot_general | solution.py:31
  269.8 0.0 reduce-scatter.5.cloned.1.call-update
  269.9 0.3 reduce-scatter.7.cloned.1.call-start
  270.1 27.3 %fusion.4 = bf16[3584,4096]{0,1:T(8,128)(2,1)} fusion(bf16[3,128,3584]{2,1,0:T(8,128)(2,1)S(1)} %copy-done.2, f32[3,4096]{1,0:T(4,128)S(1)} %copy-done.3, f32[3,128]{1,0:T(4,128)S(1)} %multiply_add_fusion, f32[3,128,4096]{2,1,0:T(8,128)} %bitcast.40, f32[3,128,4096]{2,1,0:T(8,128)} %get-tuple-element.22), kind=kOutput, calls=%fused_computation.6 | convolution fusion | flops 11296833536 | bytes 44746240 | tf_op jit(solution)/shard_map/dot_general | solution.py:44
  297.4 37.6 %copy.26 = bf16[3584,4096]{1,0:T(8,128)(2,1)} copy(bf16[3584,4096]{0,1:T(8,128)(2,1)} %fusion.4) | data formatting | bytes 58720256
  335.0 0.0 reduce-scatter.7.cloned.1.call-update
  335.1 38.6 %psum.22 = f32[]{:T(128)} all-reduce(f32[]{:T(128)} %get-tuple-element.21), channel_id=1, replica_groups=mesh['section'=16,'tensor'=2] {'section','tensor'}, use_global_device_ids=true, to_apply=%region_3.4 | all-reduce | flops 1 | bytes 8 | tf_op jit(solution)/shard_map/psum | solution.py:41
  374.3 55.6 %psum.23 = f32[3,4096]{1,0:T(4,128)S(1)} all-reduce(f32[3,4096]{1,0:T(4,128)S(1)} %get-tuple-element.20), channel_id=1, replica_groups=mesh['section'=16,'tensor'=2] {'section'}, use_global_device_ids=true, to_apply=%region_7.8 | all-reduce | flops 12288 | bytes 98304 | tf_op jit(solution)/shard_map/psum | solution.py:40
  429.9 0.6 broadcast_multiply_fusion
  430.5 0.0 reduce-scatter.5.cloned.1.call-done
  430.5 3.1 convert_element_type.42
  433.6 176.3 %reduce-scatter.7.cloned.1.call-done = bf16[224,4096]{1,0:T(8,128)(2,1)} async-done(((bf16[3584,4096]{1,0:T(8,128)(2,1)}), bf16[224,4096]{1,0:T(8,128)(2,1)}) %reduce-scatter.7.cloned.1.call-update) | async-done | bytes 1835024
  610.0 0.0 copy-start.1
  610.0 4.1 copy.27
  614.1 3.9 convert_multiply_fusion.1
  617.9 5.5 copy.24
  623.4 0.0 copy-done.1
  (3 shorter events, 0.0 us)
Async XLA Ops:
  7.2 1.9 copy-start
  7.2 4.3 copy-start.4
  7.2 219.4 %all-gather.2.cloned.1.call-start = ((), (), s32[]{:S(2)}) async-start(), calls=%async_computation.3 | async-start | bytes 31195136 | tf_op jit(solution)/shard_map/all_gather | solution.py:20
  7.9 422.6 %reduce-scatter.5.cloned.1.call-start = ((), (), s32[]{:S(2)}) async-start(), calls=%async_computation.4 | async-start | bytes 4128768 | tf_op jit(solution)/shard_map/reduce_scatter | solution.py:34
  125.5 101.0 %copy-start.2 = (bf16[3,128,3584]{2,1,0:T(8,128)(2,1)S(1)}, bf16[3,128,3584]{2,1,0:T(8,128)(2,1)}, u32[]{:S(2)}) copy-start(bf16[3,128,3584]{2,1,0:T(8,128)(2,1)} %param.6) | copy-start | bytes 8257540
  125.6 101.0 %copy-start.3 = (f32[3,4096]{1,0:T(4,128)S(1)}, f32[3,4096]{1,0:T(4,128)}, u32[]{:S(2)}) copy-start(f32[3,4096]{1,0:T(4,128)} %param.8) | copy-start | bytes 147460
  269.9 340.1 %reduce-scatter.7.cloned.1.call-start = ((), (), s32[]{:S(2)}) async-start(), calls=%async_computation.5 | async-start | bytes 31195136
  610.0 13.5 %copy-start.1 = (bf16[3,128,4096]{2,1,0:T(8,128)(2,1)S(1)}, bf16[3,128,4096]{2,1,0:T(8,128)(2,1)}, u32[]{:S(2)}) copy-start(bf16[3,128,4096]{2,1,0:T(8,128)(2,1)} %param.5) | copy-start | bytes 9437188
Sparse Core Ops, SparseCore 0:
  9.6 216.9 all-gather.1
  270.0 38.0 reduce-scatter.4
  335.2 274.7 reduce-scatter.6
where the time goes:
time: 636 us; the launch traced here: 631 us
  waiting for transfers between devices  267 us (42%)
  blocking collectives  209 us (33%)
  matrix products  70.5 us (11%)
  local copies, waits for them, and re-layouts  56.3 us (9%)
  between operations  15.6 us (2%)
  other arithmetic  12.2 us (2%)
    unnamed x4, waiting for transfers between devices  177 us
    all_to_all x1, blocking collectives, body(): lax.all_to_all(outgoing, 'section', split_axis=1, concat_axis=3, tiled=True)  110 us
    all_gather x1, waiting for transfers between devices, body(): whole_proj = lax.all_gather(proj, 'section', axis=0, tiled=True)  89.6 us
    psum x1, blocking collectives, body(): grad_gains = lax.psum(jnp.sum(ratio * pred, axis=1), 'section') * rescale  55.6 us
    unnamed x13, local copies, waits for them, and re-layouts  47.5 us
    psum x1, blocking collectives, body(): lax.psum(jnp.sum(diff * ratio), ('section', 'tensor'))  38.6 us
    dot_general x1, matrix products, body(): lax.dot_general(flat_student, flat_steer, (((0,), (0,)), ((), ())), prefe...  27.3 us
    dot_general x1, matrix products, body(): lax.dot_general(flat_steer, whole_proj, (((1,), (1,)), ((), ())), preferr...  22.4 us
  transfers between devices with their start and end apart: 3, of which 2 were waited for; matrix products, arithmetic and copies ran while one was open for 13% of the time, Pallas kernels for 0%

commit v1 on v0

--- a/solution.py
+++ b/solution.py
@@ -1,7 +1,131 @@
+import functools
+
 import jax
 import jax.numpy as jnp
 from jax import lax
+from jax.experimental import pallas as pl
+from jax.experimental.pallas import tpu as pltpu
 from jax.sharding import PartitionSpec as P
+
+MESH = pl.DeviceIdType.MESH
+SUBS = 2
+
+
+def ring_place(index, n):
+    chip, core = index // 2, index % 2
+    if n == 16:
+        z, x = chip // 2, chip % 2
+        place = z + x * (7 - 2 * z)
+    else:
+        a, b = chip // 4, chip % 4
+        place = a * 4 + b + (a % 2) * (3 - 2 * b)
+    return place * 2 + core
+
+
+def ring_index(place, n):
+    spot, core = place // 2, place % 2
+    if n == 16:
+        x = spot // 4
+        z = spot + x * (7 - 2 * spot)
+        chip = z * 2 + x
+    else:
+        a, b = spot // 4, spot % 4
+        chip = a * 4 + b + (a % 2) * (3 - 2 * b)
+    return chip * 2 + core
+
+
+def reduce_kernel(n, rescale, st_ref, steer_ref, out_ref, slots, send_sem, recv_sem):
+    tensor = lax.axis_index("tensor")
+    me = ring_place(lax.axis_index("section"), n)
+    right = ring_index((me + 1) % n, n)
+    left = ring_index((me + n - 1) % n, n)
+    towards = (right, left)
+    wide = slots.shape[-1]
+
+    barrier = pltpu.get_barrier_semaphore()
+    for neighbour in towards:
+        pl.semaphore_signal(barrier, inc=1, device_id=(neighbour, tensor), device_id_type=MESH)
+    pl.semaphore_wait(barrier, 2)
+
+    def columns(d, j):
+        return pl.ds((d * SUBS + j) * wide, wide)
+
+    def term(d, j, step):
+        place = (me + 2 * n - 1 - step) % n if d == 0 else (me + 1 + step) % n
+        return jnp.dot(
+            st_ref[ring_index(place, n)],
+            steer_ref[:, columns(d, j)],
+            preferred_element_type=jnp.float32,
+        )
+
+    def copy(d, j, step):
+        return pltpu.make_async_remote_copy(
+            src_ref=slots.at[d, j, step],
+            dst_ref=slots.at[d, j, step + 1],
+            send_sem=send_sem.at[d, j, step],
+            recv_sem=recv_sem.at[d, j, step],
+            device_id=(towards[d], tensor),
+            device_id_type=MESH,
+        )
+
+    for j in range(SUBS):
+        for d in range(2):
+            slots[d, j, 0] = term(d, j, 0).astype(jnp.bfloat16)
+            copy(d, j, 0).start()
+
+    def body(step, carry):
+        for j in range(SUBS):
+            for d in range(2):
+                own = term(d, j, step)
+                copy(d, j, step - 1).wait_recv()
+                slots[d, j, step] = (slots[d, j, step].astype(jnp.float32) + own).astype(
+                    jnp.bfloat16
+                )
+                copy(d, j, step).start()
+        return carry
+
+    lax.fori_loop(1, n - 1, body, 0)
+    for j in range(SUBS):
+        for d in range(2):
+            own = term(d, j, n - 1)
+            copy(d, j, n - 2).wait_recv()
+            out_ref[:, columns(d, j)] = (
+                slots[d, j, n - 1].astype(jnp.float32) + own
+            ) * rescale
+
+    def drain(step, carry):
+        for j in range(SUBS):
+            for d in range(2):
+                copy(d, j, step).wait_send()
+        return carry
+
+    lax.fori_loop(0, n - 1, drain, 0)
+
+
+def reduce_terms(student_blocks, steer, n, rescale):
+    rows = student_blocks.shape[1]
+    width = steer.shape[1]
+    wide = width // (2 * SUBS)
+    return pl.pallas_call(
+        functools.partial(reduce_kernel, n, rescale),
+        out_shape=jax.ShapeDtypeStruct((rows, width), jnp.float32),
+        in_specs=[pl.BlockSpec(memory_space=pltpu.VMEM)] * 2,
+        out_specs=pl.BlockSpec(memory_space=pltpu.VMEM),
+        scratch_shapes=[
+            pltpu.VMEM((2, SUBS, n, rows, wide), jnp.bfloat16),
+            pltpu.SemaphoreType.DMA((2, SUBS, n)),
+            pltpu.SemaphoreType.DMA((2, SUBS, n)),
+        ],
+        compiler_params=pltpu.CompilerParams(
+            collective_id=0, has_side_effects=True, vmem_limit_bytes=52 * 1024 * 1024
+        ),
+        cost_estimate=pl.CostEstimate(
+            flops=2 * n * rows * width * steer.shape[0],
+            bytes_accessed=400_000_000,
+            transcendentals=0,
+        ),
+        name="reduce_terms",
+    )(student_blocks, steer)
 
 
 def body(section_rows, student_rows, proj, gains, offsets):
@@ -19,6 +143,7 @@
     target = incoming.reshape(3, seq_dev, width).astype(jnp.float32)
     whole_proj = lax.all_gather(proj, "section", axis=0, tiled=True)
     flat_student = student_rows.reshape(3 * seq_dev, student_width)
+    student_blocks = flat_student.T.reshape(sections, student_width // sections, 3 * seq_dev)
     pred = jnp.dot(flat_student, whole_proj, preferred_element_type=jnp.float32).reshape(
         3, seq_dev, width
     )
@@ -37,19 +162,13 @@
         scatter_dimension=2,
         tiled=True,
     ).astype(jnp.float32)
-    grad_gains = lax.psum(jnp.sum(ratio * pred, axis=1), "section") * rescale
-    loss = lax.psum(jnp.sum(diff * ratio), ("section", "tensor")) / (
-        2.0 * total_rows * width * tensors
+    sums = jnp.concatenate(
+        [jnp.sum(ratio * pred, axis=1), jnp.sum(diff * ratio, axis=(0, 1))[None]], axis=0
     )
-    term = lax.dot_general(
-        flat_student, flat_steer, (((0,), (0,)), ((), ())), preferred_element_type=jnp.float32
-    )
-    grad_proj = (
-        lax.psum_scatter(
-            term.astype(jnp.bfloat16), "section", scatter_dimension=0, tiled=True
-        ).astype(jnp.float32)
-        * rescale
-    )
+    sums = lax.psum(sums, "section")
+    grad_gains = sums[:3] * rescale
+    loss = lax.psum(jnp.sum(sums[3]), "tensor") / (2.0 * total_rows * width * tensors)
+    grad_proj = reduce_terms(student_blocks, flat_steer, sections, rescale)
     return (loss, grad_student, grad_proj, grad_gains)
 
 

time: 636 us -> 452 us (0.71)
  waiting for transfers between devices: 267 us -> 90.5 us
  Pallas kernels: 0 us -> 159 us
  blocking collectives: 209 us -> 121 us
  local copies, waits for them, and re-layouts: 56.3 us -> 15.5 us
  matrix products: 70.5 us -> 39.4 us
    unnamed x4 -> x3, waiting for transfers between devices: 177 us -> 0.71 us
    pallas_call x0 -> x1, Pallas kernels: none -> 159 us  [reduce_terms(): pl.pallas_call(functools.partial(reduce_kernel, n, rescale), out_shape=ja...]
    psum x2 -> x1, blocking collectives: 94.2 us -> 5.55 us  [body(): lax.psum(jnp.sum(sums[3]), 'tensor') / (2.0 * total_rows * width * tensors)]
    unnamed x13, local copies, waits for them, and re-layouts: 47.5 us -> 3.9 us
    dot_general x1 -> x0, matrix products: 27.3 us -> none  [body(): lax.dot_general(flat_student, flat_steer, (((0,), (0,)), ((), ())), prefe...]
  transfers between devices with their start and end apart: 3 -> 3, of which waited for: 2 -> 1; matrix products, arithmetic and copies ran while one was open for 13% -> 8% of each run, Pallas kernels for 0% -> 35%
where the time goes in v1:
time: 452 us
  Pallas kernels  159 us (35%)
  blocking collectives  121 us (27%)
  waiting for transfers between devices  90.5 us (20%)
  matrix products  39.4 us (9%)
  between operations  15.6 us (3%)
  local copies, waits for them, and re-layouts  15.5 us (3%)
  other arithmetic  11.4 us (3%)
    pallas_call x1, Pallas kernels, reduce_terms(): pl.pallas_call(functools.partial(reduce_kernel, n, rescale), out_shape=ja...  159 us
    all_to_all x1, blocking collectives, body(): lax.all_to_all(outgoing, 'section', split_axis=1, concat_axis=3, tiled=True)  110 us
    all_gather x1, waiting for transfers between devices, body(): whole_proj = lax.all_gather(proj, 'section', axis=0, tiled=True)  89.8 us
    dot_general x1, matrix products, body(): jnp.dot(flat_student, whole_proj, preferred_element_type=jnp.float32)  20.8 us
    dot_general x1, matrix products, body(): lax.dot_general(flat_steer, whole_proj, (((1,), (1,)), ((), ())), preferr...  18.6 us
  transfers between devices with their start and end apart: 3, of which 1 were waited for; matrix products, arithmetic and copies ran while one was open for 8% of the time, Pallas kernels for 35%

profile of v1, /device:TPU:8, one launch (start us, length us, event | category | flops | bytes accessed | tf_op | source)
XLA Modules:
  0.0 452.0 jit_solution(3867102859647700850)
XLA Ops:
  7.2 0.0 copy-start
  7.2 0.0 all-gather.2.cloned.1.call-start
  7.2 0.7 all-gather.2.cloned.1.call-update
  7.9 0.0 all-reduce.2.cloned.1.call-start
  8.0 0.8 compare_select_fusion
  8.8 0.3 copy-done
  9.1 0.0 copy-start.5
  9.1 2.4 gather_fusion
  11.5 0.0 copy-done.5
  11.5 2.3 fusion.9
  13.7 110.2 %all_to_all.4 = bf16[3,16,8,1,4096]{4,2,0,3,1:T(8,128)(2,1)S(1)} all-to-all(bf16[3,16,8,1,4096]{4,2,0,3,1:T(8,128)(2,1)S(1)} %fusion.9), channel_id=1, replica_groups=mesh['section'=16,'tensor'=2] {'section'}, dimensions={1} | all-to-all | bytes 6291456 | tf_op jit(solution)/shard_map/all_to_all | solution.py:142
  123.9 0.8 convert_bitcast_fusion
  124.7 6.3 %copy.17 = f32[3,1,8,16,1,4096]{5,3,2,0,4,1:T(8,128)} copy(f32[3,1,8,16,1,4096]{5,2,0,3,4,1:T(8,128)S(1)} %convert_bitcast_fusion) | data formatting | bytes 12582912 | tf_op jit(solution)/shard_map/convert_element_type | solution.py:143
  131.0 0.0 copy-start.4
  131.0 0.7 fusion.5
  131.7 0.1 copy.19
  131.7 0.1 reduce_sum.42
  131.8 4.9 %psum.21 = f32[3,128]{1,0:T(4,128)S(1)} all-reduce(f32[3,128]{1,0:T(4,128)S(1)} %reduce_sum.42), channel_id=1, replica_groups=mesh['section'=16,'tensor'=2] {'tensor'}, use_global_device_ids=true, to_apply=%region_1.2 | all-reduce | flops 384 | bytes 3072 | tf_op jit(solution)/shard_map/psum | solution.py:151
  136.8 89.8 %all-gather.2.cloned.1.call-done = bf16[3584,4096]{1,0:T(8,128)(2,1)} async-done(((bf16[224,4096]{1,0:T(8,128)(2,1)}), bf16[3584,4096]{1,0:T(8,128)(2,1)}) %all-gather.2.cloned.1.call-update) | async-done | bytes 29360144 | tf_op jit(solution)/shard_map/all_gather | solution.py:144
  226.6 0.0 copy-done.4
  226.6 20.8 %multiply_reduce_fusion.1 = (f32[3,4096]{1,0:T(4,128)S(1)}, f32[4096]{0:T(1024)S(1)}, bf16[3,128,4096]{2,1,0:T(8,128)(2,1)}) fusion(f32[3,128]{1,0:T(4,128)S(1)} %multiply_add_fusion, f32[3,128,4096]{2,1,0:T(8,128)} %bitcast.37, f32[3,4096]{1,0:T(4,128)S(1)} %copy-done.4, bf16[3,128,3584]{2,1,0:T(8,128)(2,1)} %param.6, ...), kind=kOutput, calls=%fused_computation.11 | convolution fusion | flops 11288428544 | bytes 41666048 | tf_op jit(solution)/shard_map/dot_general | solution.py:147
  247.4 0.7 pad_maximum_fusion
  248.1 0.0 all-reduce.2.cloned.1.call-update
  248.1 0.2 reduce-scatter.2.cloned.1.call-start
  248.3 18.6 %fusion.6 = bf16[3,128,3584]{2,1,0:T(8,128)(2,1)} fusion(bf16[3,128,4096]{2,1,0:T(8,128)(2,1)} %get-tuple-element.6, bf16[3584,4096]{1,0:T(8,128)(2,1)} %all-gather.2.cloned.1.call-done), kind=kOutput, calls=%fused_computation.13 | convolution fusion | flops 11275665408 | bytes 35258368 | tf_op jit(solution)/shard_map/dot_general | solution.py:156
  266.9 0.0 copy-start.3
  266.9 0.0 reduce-scatter.2.cloned.1.call-update
  266.9 1.8 copy-done.3
  268.7 2.7 copy.20
  271.4 158.6 %reduce_terms.1 = f32[224,4096]{1,0:T(8,128)} custom-call(bf16[16,224,384]{2,1,0:T(8,128)(2,1)} %bitcast.39, bf16[384,4096]{1,0:T(8,128)(2,1)} %bitcast.42), custom_call_target="tpu_custom_call" | custom-call | flops 11274289152 | bytes 400000000 | tf_op jit(solution)/shard_map/reduce_terms/pallas_call | solution.py:109
  430.1 0.0 all-reduce.2.cloned.1.call-done
  430.1 1.5 slice_reduce_fusion
  431.6 5.5 %psum.23 = f32[]{:T(128)} all-reduce(f32[]{:T(128)} %slice_reduce_fusion), channel_id=1, replica_groups=mesh['section'=16,'tensor'=2] {'tensor'}, use_global_device_ids=true, to_apply=%region_6.7 | all-reduce | flops 1 | bytes 8 | tf_op jit(solution)/shard_map/psum | solution.py:170
  437.8 1.5 slice_multiply_fusion
  439.3 0.0 reduce-scatter.2.cloned.1.call-done
  439.3 0.0 copy-start.2
  439.3 0.0 copy-start.1
  439.3 3.2 convert_element_type.33
  442.5 0.0 copy-done.2
  442.5 1.8 copy.23
  444.3 0.0 copy-done.1
  (3 shorter events, 0.0 us)
Async XLA Ops:
  7.2 1.9 copy-start
  7.2 219.4 %all-gather.2.cloned.1.call-start = ((), (), s32[]{:S(2)}) async-start(), calls=%async_computation.2 | async-start | bytes 31195136 | tf_op jit(solution)/shard_map/all_gather | solution.py:144
  7.9 422.2 %all-reduce.2.cloned.1.call-start = ((), (), s32[]{:S(2)}) async-start(), calls=%async_computation.3 | async-start | bytes 131072 | tf_op jit(solution)/shard_map/psum | solution.py:168
  9.1 2.4 copy-start.5
  131.0 95.6 %copy-start.4 = (f32[3,4096]{1,0:T(4,128)S(1)}, f32[3,4096]{1,0:T(4,128)}, u32[]{:S(2)}) copy-start(f32[3,4096]{1,0:T(4,128)} %param.8) | copy-start | bytes 147460
  248.1 191.2 %reduce-scatter.2.cloned.1.call-start = ((), (), s32[]{:S(2)}) async-start(), calls=%async_computation.4 | async-start | bytes 4128768 | tf_op jit(solution)/shard_map/reduce_scatter | solution.py:159
  266.9 1.8 copy-start.3
  439.3 3.2 copy-start.2
  439.3 5.1 %copy-start.1 = (bf16[3,128,4096]{2,1,0:T(8,128)(2,1)S(1)}, bf16[3,128,4096]{2,1,0:T(8,128)(2,1)}, u32[]{:S(2)}) copy-start(bf16[3,128,4096]{2,1,0:T(8,128)(2,1)} %param.5) | copy-start | bytes 9437188
Sparse Core Ops, SparseCore 0:
  9.6 216.9 all-gather.1
  248.2 87.0 all-reduce.1
  338.2 38.1 reduce-scatter.1

commit v2 on v1

--- a/solution.py
+++ b/solution.py
@@ -128,6 +128,156 @@
     )(student_blocks, steer)
 
 
+def gather_kernel(n, proj_ref, student_ref, outgoing_ref, whole_ref, pred_ref, target_ref,
+                  slots, send_sem, recv_sem, keep_sem, out_sem, in_sem, own_sem):
+    tensor = lax.axis_index("tensor")
+    index = lax.axis_index("section")
+    me = ring_place(index, n)
+    towards = (ring_index((me + 1) % n, n), ring_index((me + n - 1) % n, n))
+    rows, wide = slots.shape[-2:]
+
+    barrier = pltpu.get_barrier_semaphore()
+    for s in range(1, n):
+        pl.semaphore_signal(
+            barrier, inc=1, device_id=((index + s) % n, tensor), device_id_type=MESH
+        )
+    pl.semaphore_wait(barrier, n - 1)
+
+    def columns(d, j):
+        return pl.ds((d * SUBS + j) * wide, wide)
+
+    def owner(d, step):
+        return ring_index((me + n - step) % n if d == 0 else (me + step) % n, n)
+
+    def copy(d, j, step):
+        return pltpu.make_async_remote_copy(
+            src_ref=slots.at[d, j, step],
+            dst_ref=slots.at[d, j, step + 1],
+            send_sem=send_sem.at[d, j, step],
+            recv_sem=recv_sem.at[d, j, step],
+            device_id=(towards[d], tensor),
+            device_id_type=MESH,
+        )
+
+    def keep(d, j, step):
+        place = pl.ds(pl.multiple_of(owner(d, step) * rows, 16), rows)
+        return pltpu.make_async_copy(
+            slots.at[d, j, step], whole_ref.at[place, columns(d, j)], keep_sem.at[d, j, step]
+        )
+
+    def teach(s):
+        there = (index + s) % n
+        return pltpu.make_async_remote_copy(
+            src_ref=outgoing_ref.at[there],
+            dst_ref=target_ref.at[index],
+            send_sem=out_sem.at[s],
+            recv_sem=in_sem.at[index],
+            device_id=(there, tensor),
+            device_id_type=MESH,
+        )
+
+    def taught(s):
+        source = (index + n - s) % n
+        return pltpu.make_async_remote_copy(
+            src_ref=outgoing_ref.at[source],
+            dst_ref=target_ref.at[source],
+            send_sem=out_sem.at[s],
+            recv_sem=in_sem.at[source],
+            device_id=(source, tensor),
+            device_id_type=MESH,
+        )
+
+    def product(d, j, step):
+        return jnp.dot(
+            student_ref[owner(d, step)], slots[d, j, step], preferred_element_type=jnp.float32
+        )
+
+    for j in range(SUBS):
+        for d in range(2):
+            slots[d, j, 0] = proj_ref[:, columns(d, j)]
+            copy(d, j, 0).start()
+    own = pltpu.make_async_copy(outgoing_ref.at[index], target_ref.at[index], own_sem)
+    own.start()
+    teach(1).start()
+    for j in range(SUBS):
+        for d in range(2):
+            keep(d, j, 0).start()
+            pred_ref[:, columns(d, j)] = product(d, j, 0)
+
+    def body(step, carry):
+        teach(step + 1).start()
+        for j in range(SUBS):
+            for d in range(2):
+                copy(d, j, step - 1).wait_recv()
+                copy(d, j, step).start()
+                keep(d, j, step).start()
+                pred_ref[:, columns(d, j)] += product(d, j, step)
+        return carry
+
+    lax.fori_loop(1, n - 1, body, 0)
+    for j in range(SUBS):
+        for d in range(2):
+            copy(d, j, n - 2).wait_recv()
+            keep(d, j, n - 1).start()
+            pred_ref[:, columns(d, j)] += product(d, j, n - 1)
+
+    own.wait()
+
+    def drain(step, carry):
+        for j in range(SUBS):
+            for d in range(2):
+                copy(d, j, step).wait_send()
+                keep(d, j, step).wait()
+        teach(step + 1).wait_send()
+        taught(step + 1).wait_recv()
+        return carry
+
+    lax.fori_loop(0, n - 1, drain, 0)
+    for j in range(SUBS):
+        for d in range(2):
+            keep(d, j, n - 1).wait()
+
+
+def gather_project(proj, student_blocks, outgoing):
+    n, tokens, rows = student_blocks.shape
+    width = proj.shape[1]
+    wide = width // (2 * SUBS)
+    return pl.pallas_call(
+        functools.partial(gather_kernel, n),
+        out_shape=(
+            jax.ShapeDtypeStruct((n * rows, width), jnp.bfloat16),
+            jax.ShapeDtypeStruct((tokens, width), jnp.float32),
+            jax.ShapeDtypeStruct(outgoing.shape, jnp.bfloat16),
+        ),
+        in_specs=[
+            pl.BlockSpec(memory_space=pltpu.VMEM),
+            pl.BlockSpec(memory_space=pltpu.VMEM),
+            pl.BlockSpec(memory_space=pl.ANY),
+        ],
+        out_specs=(
+            pl.BlockSpec(memory_space=pl.ANY),
+            pl.BlockSpec(memory_space=pltpu.VMEM),
+            pl.BlockSpec(memory_space=pl.ANY),
+        ),
+        scratch_shapes=[
+            pltpu.VMEM((2, SUBS, n, rows, wide), jnp.bfloat16),
+            pltpu.SemaphoreType.DMA((2, SUBS, n)),
+            pltpu.SemaphoreType.DMA((2, SUBS, n)),
+            pltpu.SemaphoreType.DMA((2, SUBS, n)),
+            pltpu.SemaphoreType.DMA((n,)),
+            pltpu.SemaphoreType.DMA((n,)),
+            pltpu.SemaphoreType.DMA,
+        ],
+        compiler_params=pltpu.CompilerParams(
+            collective_id=1, has_side_effects=True, vmem_limit_bytes=52 * 1024 * 1024
+        ),
+        cost_estimate=pl.CostEstimate(
+            flops=2 * n * rows * width * tokens, bytes_accessed=500_000_000, transcendentals=0
+        ),
+        name="gather_project",
+    )(proj, student_blocks, outgoing)
+
+
 def body(section_rows, student_rows, proj, gains, offsets):
     sections = lax.axis_size("section")
     tensors = lax.axis_size("tensor")
@@ -137,33 +287,44 @@
     per_source = seq_dev // sections
     total_rows = 3 * seq_dev * sections
     rescale = float(total_rows) ** (-0.5)
-    blocks = section_rows.reshape(3, sections, per_source, 1, width)
-    outgoing = jnp.take(blocks, offsets, axis=1)
-    incoming = lax.all_to_all(outgoing, "section", split_axis=1, concat_axis=3, tiled=True)
-    target = incoming.reshape(3, seq_dev, width).astype(jnp.float32)
-    whole_proj = lax.all_gather(proj, "section", axis=0, tiled=True)
-    flat_student = student_rows.reshape(3 * seq_dev, student_width)
-    student_blocks = flat_student.T.reshape(sections, student_width // sections, 3 * seq_dev)
-    pred = jnp.dot(flat_student, whole_proj, preferred_element_type=jnp.float32).reshape(
-        3, seq_dev, width
-    )
+    parts = sections // 8
+    part = width // parts
+    per_rank = 3 * per_source
+    blocks = section_rows.reshape(3, sections, per_source, width)
+    outgoing = jnp.take(blocks, offsets, axis=1).transpose(1, 0, 2, 3)
+    outgoing = outgoing.reshape(sections, per_rank, width)
+    outgoing = jnp.concatenate(
+        [outgoing[:, :, c * part : (c + 1) * part] for c in range(parts)], axis=1
+    )
+    ordered = student_rows.reshape(3, per_source, sections, student_width).transpose(2, 0, 1, 3)
+    flat_student = ordered.reshape(3 * seq_dev, student_width)
+    section_depth = student_width // sections
+    student_blocks = flat_student.T.reshape(sections, section_depth, 3 * seq_dev)
+    student_left = student_blocks.transpose(0, 2, 1)
+    whole_proj, pred, incoming = gather_project(proj, student_left, outgoing)
+    shape = (sections, 3, per_source, width)
+    pred = pred.reshape(shape)
+    target = jnp.concatenate(
+        [incoming[:, c * per_rank : (c + 1) * per_rank] for c in range(parts)], axis=2
+    )
+    target = target.reshape(shape).astype(jnp.float32)
     squares = jnp.sum(target * target, axis=-1)
     scale = lax.psum(squares, "tensor") / (width * tensors) + 1e-06
-    diff = gains[:, None, :] * pred - target
-    ratio = diff / scale[:, :, None]
-    steer = (gains[:, None, :] * ratio).astype(jnp.bfloat16)
+    gain = gains[None, :, None, :]
+    diff = gain * pred - target
+    ratio = diff / scale[..., None]
+    steer = (gain * ratio).astype(jnp.bfloat16)
     flat_steer = steer.reshape(3 * seq_dev, width)
     partial_student = lax.dot_general(
         flat_steer, whole_proj, (((1,), (1,)), ((), ())), preferred_element_type=jnp.float32
     )
     grad_student = lax.psum_scatter(
-        partial_student.reshape(3, seq_dev, student_width).astype(jnp.bfloat16),
-        "tensor",
-        scatter_dimension=2,
-        tiled=True,
-    ).astype(jnp.float32)
+        partial_student.astype(jnp.bfloat16), "tensor", scatter_dimension=1, tiled=True
+    )
+    grad_student = grad_student.reshape(sections, 3, per_source, student_width // tensors)
+    grad_student = grad_student.transpose(1, 2, 0, 3).reshape(3, seq_dev, -1).astype(jnp.float32)
     sums = jnp.concatenate(
-        [jnp.sum(ratio * pred, axis=1), jnp.sum(diff * ratio, axis=(0, 1))[None]], axis=0
+        [jnp.sum(ratio * pred, axis=(0, 2)), jnp.sum(diff * ratio, axis=(0, 1, 2))[None]], axis=0
     )
     sums = lax.psum(sums, "section")
     grad_gains = sums[:3] * rescale

time: 452 us -> 490 us (1.084)
  Pallas kernels: 159 us -> 386 us
  blocking collectives: 121 us -> 13.7 us
  waiting for transfers between devices: 90.5 us -> 0.06 us
  matrix products: 39.4 us -> 17.2 us
  other arithmetic: 11.4 us -> 25.1 us
  local copies, waits for them, and re-layouts: 15.5 us -> 27.5 us
    pallas_call x0 -> x1, Pallas kernels: none -> 221 us  [gather_project(): pl.pallas_call(functools.partial(gather_kernel, n), out_shape=(jax.ShapeD...]
    all_to_all x1 -> x0, blocking collectives: 110 us -> none  [body(): lax.all_to_all(outgoing, 'section', split_axis=1, concat_axis=3, tiled=True)]
    all_gather x1 -> x0, waiting for transfers between devices: 89.8 us -> none  [body(): whole_proj = lax.all_gather(proj, 'section', axis=0, tiled=True)]
    dot_general x1 -> x0, matrix products: 20.8 us -> none  [body(): jnp.dot(flat_student, whole_proj, preferred_element_type=jnp.float32)]
    transpose x0 -> x3, local copies, waits for them, and re-layouts: none -> 13.9 us  [the longest x1 4.82 us: body(): student_rows.reshape(3, per_source, sections, student_width)]
    pallas_call x1, Pallas kernels: 159 us -> 165 us  [reduce_terms(): pl.pallas_call(functools.partial(reduce_kernel, n, rescale), out_shape=ja...]
    convert_element_type x2 -> x3, other arithmetic: 3.99 us -> 8.94 us  [the longest x1 4.08 us: body(): steer = (gain * ratio).astype(jnp.bfloat16)]
  transfers between devices with their start and end apart: 3 -> 2, of which waited for: 1 -> 0; matrix products, arithmetic and copies ran while one was open for 8% -> 4% of each run, Pallas kernels for 35% -> 34%
where the time goes in v2:
time: 490 us; the launch traced here: 488 us
  Pallas kernels  386 us (79%)
  local copies, waits for them, and re-layouts  27.5 us (6%)
  other arithmetic  25.1 us (5%)
  between operations  17.4 us (4%)
  matrix products  17.2 us (4%)
  blocking collectives  13.7 us (3%)
    pallas_call x1, Pallas kernels, gather_project(): pl.pallas_call(functools.partial(gather_kernel, n), out_shape=(jax.ShapeD...  221 us
    pallas_call x1, Pallas kernels, reduce_terms(): pl.pallas_call(functools.partial(reduce_kernel, n, rescale), out_shape=ja...  165 us
    dot_general x1, matrix products, body(): lax.dot_general(flat_steer, whole_proj, (((1,), (1,)), ((), ())), preferr...  17.2 us
  transfers between devices with their start and end apart: 2, of which 0 were waited for; matrix products, arithmetic and copies ran while one was open for 4% of the time, Pallas kernels for 34%

profile of v2, /device:TPU:8, one launch (start us, length us, event | category | flops | bytes accessed | tf_op | source)
XLA Modules:
  0.0 487.5 jit_solution(5675471405960788541)
XLA Ops:
  8.0 0.0 copy-start
  8.0 0.0 all-reduce.2.cloned.1.call-start
  8.1 0.8 compare_and_fusion
  8.9 0.8 compare_select_fusion
  9.6 4.8 copy.23
  14.5 4.5 copy.24
  19.0 0.0 copy-done
  19.0 2.4 gather_fusion
  21.4 2.3 select_bitcast_fusion
  23.7 2.1 fusion.6
  25.7 4.6 copy.25.student_ref
  30.3 0.0 copy-start.2
  30.3 4.1 pad_maximum_fusion.outgoing_ref
  34.4 0.0 copy-done.2
  34.4 221.4 %gather_project.1 = (bf16[3584,4096]{1,0:T(8,128)(2,1)}, f32[384,4096]{1,0:T(8,128)}, bf16[16,48,2048]{2,1,0:T(8,128)(2,1)}) custom-call(bf16[224,4096]{1,0:T(8,128)(2,1)S(1)} %copy-done.2, bf16[16,384,224]{2,1,0:T(8,128)(2,1)} %copy.25.student_ref, bf16[16,48,2048]{2,1,0:T(8,128)(2,1)} %pad_maximum_fusion.outgoing_ref), custom_call_target="tpu_custom_call" | custom-call | flops 11274289152 | bytes 500000000 | tf_op jit(solution)/shard_map/gather_project/pallas_call | solution.py:245
  255.8 2.3 fusion.5
  258.1 0.7 multiply_reduce_fusion.1
  258.8 0.0 copy-start.6
  258.8 3.3 maximum_convert_fusion
  262.2 0.1 copy.26
  262.2 8.1 %psum.21 = f32[16,3,8]{0,2,1:T(8,128)S(1)} all-reduce(f32[16,3,8]{0,2,1:T(8,128)S(1)} %bitcast.56), channel_id=1, replica_groups=mesh['section'=16,'tensor'=2] {'tensor'}, use_global_device_ids=true, to_apply=%region_1.2 | all-reduce | flops 384 | bytes 3072 | tf_op jit(solution)/shard_map/psum | solution.py:312
  270.4 0.1 copy.27
  270.4 0.1 div.29
  270.5 0.0 copy-done.6
  270.5 0.0 copy-start.3
  270.6 3.8 fusion.4
  274.3 0.9 copy-done.3
  275.2 4.1 fusion.1
  279.3 0.0 copy-start.5
  279.3 0.8 pad_maximum_fusion.1
  280.0 0.0 all-reduce.2.cloned.1.call-update
  280.1 0.2 reduce-scatter.2.cloned.1.call-start
  280.3 17.2 %convolution_convert_fusion = bf16[384,3584]{1,0:T(8,128)(2,1)} fusion(bf16[384,4096]{1,0:T(8,128)(2,1)S(1)} %get-tuple-element.10.steer_ref, bf16[3584,4096]{1,0:T(8,128)(2,1)} %get-tuple-element.9), kind=kOutput, calls=%fused_computation.11 | convolution fusion | flops 11275665408 | bytes 35258368 | tf_op jit(solution)/shard_map/dot_general | solution.py:318
  297.5 0.0 copy-done.5
  297.5 0.0 reduce-scatter.2.cloned.1.call-update
  297.5 165.0 %reduce_terms.1 = f32[224,4096]{1,0:T(8,128)} custom-call(bf16[16,224,384]{2,1,0:T(8,128)(2,1)} %bitcast.50, bf16[384,4096]{1,0:T(8,128)(2,1)} %copy-done.5), custom_call_target="tpu_custom_call" | custom-call | flops 11274289152 | bytes 400000000 | tf_op jit(solution)/shard_map/reduce_terms/pallas_call | solution.py:109
  462.5 0.0 all-reduce.2.cloned.1.call-done
  462.6 1.5 slice_reduce_fusion
  464.1 5.5 %psum.23 = f32[]{:T(128)} all-reduce(f32[]{:T(128)} %slice_reduce_fusion), channel_id=1, replica_groups=mesh['section'=16,'tensor'=2] {'tensor'}, use_global_device_ids=true, to_apply=%region_6.7 | all-reduce | flops 1 | bytes 8 | tf_op jit(solution)/shard_map/psum | solution.py:331
  470.3 1.5 slice_multiply_fusion
  471.7 0.0 reduce-scatter.2.cloned.1.call-done
  471.7 1.5 convert_bitcast_fusion
  473.3 0.0 copy-start.4
  473.3 2.4 copy.29
  475.6 0.0 copy-start.1
  475.6 0.3 copy-done.4
  475.9 1.9 copy.32
  477.8 1.1 copy-done.1
  (2 shorter events, 0.0 us)
Async XLA Ops:
  8.0 11.0 %copy-start = (bf16[3,128,4096]{2,1,0:T(8,128)(2,1)S(1)}, bf16[3,128,4096]{2,1,0:T(8,128)(2,1)}, u32[]{:S(2)}) copy-start(bf16[3,128,4096]{2,1,0:T(8,128)(2,1)} %param.5) | copy-start | bytes 9437188
  8.0 454.6 %all-reduce.2.cloned.1.call-start = ((), (), s32[]{:S(2)}) async-start(), calls=%async_computation.1 | async-start | bytes 131072 | tf_op jit(solution)/shard_map/psum | solution.py:329
  30.3 4.1 copy-start.2
  258.8 11.7 %copy-start.6 = (f32[3,4096]{1,0:T(4,128)S(1)}, f32[3,4096]{1,0:T(4,128)}, u32[]{:S(2)}) copy-start(f32[3,4096]{1,0:T(4,128)} %param.8) | copy-start | bytes 147460
  270.5 4.6 copy-start.3
  279.3 18.2 %copy-start.5 = (bf16[384,4096]{1,0:T(8,128)(2,1)}, bf16[384,4096]{1,0:T(8,128)(2,1)S(1)}, u32[]{:S(2)}) copy-start(bf16[384,4096]{1,0:T(8,128)(2,1)S(1)} %get-tuple-element.10.steer_ref) | copy-start | bytes 9437188
  280.1 191.7 %reduce-scatter.2.cloned.1.call-start = ((), (), s32[]{:S(2)}) async-start(), calls=%async_computation.2 | async-start | bytes 4128768 | tf_op jit(solution)/shard_map/reduce_scatter | solution.py:321
  473.3 2.7 copy-start.4
  475.6 3.3 copy-start.1
Sparse Core Ops, SparseCore 0:
  280.2 94.5 all-reduce.1
Sparse Core Ops, SparseCore 1:
  297.6 45.3 reduce-scatter.1

commit v3 on v1

--- a/solution.py
+++ b/solution.py
@@ -8,7 +8,7 @@
 from jax.sharding import PartitionSpec as P
 
 MESH = pl.DeviceIdType.MESH
-SUBS = 2
+SUBS = 4
 
 
 def ring_place(index, n):
@@ -144,6 +144,7 @@
     whole_proj = lax.all_gather(proj, "section", axis=0, tiled=True)
     flat_student = student_rows.reshape(3 * seq_dev, student_width)
     student_blocks = flat_student.T.reshape(sections, student_width // sections, 3 * seq_dev)
+    whole_proj, student_blocks = lax.optimization_barrier((whole_proj, student_blocks))
     pred = jnp.dot(flat_student, whole_proj, preferred_element_type=jnp.float32).reshape(
         3, seq_dev, width
     )

time: 452 us -> 454 us (level)
  blocking collectives: 121 us -> 10.7 us
  waiting for transfers between devices: 90.5 us -> 188 us
  other arithmetic: 11.4 us -> 26.2 us
  starting transfers between devices: 0.3 us -> 6.6 us
  local copies, waits for them, and re-layouts: 15.5 us -> 9.31 us
    all_to_all x1 -> x0, blocking collectives: 110 us -> none  [body(): lax.all_to_all(outgoing, 'section', split_axis=1, concat_axis=3, tiled=True)]
    all_to_all x0 -> x1, waiting for transfers between devices: none -> 99.5 us  [body(): lax.all_to_all(outgoing, 'section', split_axis=1, concat_axis=3, tiled=True)]
    reduce_sum x0 -> x1, other arithmetic: none -> 6.72 us  [body(): jnp.sum(ratio * pred, axis=1)]
    convert_element_type x1 -> x0, local copies, waits for them, and re-layouts: 6.28 us -> none  [body(): target = incoming.reshape(3, seq_dev, width).astype(jnp.float32)]
    all_to_all x0 -> x1, starting transfers between devices: none -> 6.27 us  [body(): lax.all_to_all(outgoing, 'section', split_axis=1, concat_axis=3, tiled=True)]
  transfers between devices with their start and end apart: 3 -> 4, of which waited for: 1 -> 2; matrix products, arithmetic and copies ran while one was open for 8% -> 9% of each run, Pallas kernels for 35% -> 35%
where the time goes in v3:
time: 454 us
  waiting for transfers between devices  188 us (41%)
  Pallas kernels  160 us (35%)
  matrix products  38 us (8%)
  other arithmetic  26.2 us (6%)
  between operations  15.6 us (3%)
  blocking collectives  10.7 us (2%)
  local copies, waits for them, and re-layouts  9.31 us (2%)
  starting transfers between devices  6.6 us (1%)
    pallas_call x1, Pallas kernels, reduce_terms(): pl.pallas_call(functools.partial(reduce_kernel, n, rescale), out_shape=ja...  160 us
    all_to_all x1, waiting for transfers between devices, body(): lax.all_to_all(outgoing, 'section', split_axis=1, concat_axis=3, tiled=True)  99.5 us
    all_gather x1, waiting for transfers between devices, body(): whole_proj = lax.all_gather(proj, 'section', axis=0, tiled=True)  87.6 us
    dot_general x1, matrix products, body(): jnp.dot(flat_student, whole_proj, preferred_element_type=jnp.float32)  20.9 us
    dot_general x1, matrix products, body(): lax.dot_general(flat_steer, whole_proj, (((1,), (1,)), ((), ())), preferr...  17.2 us
  transfers between devices with their start and end apart: 4, of which 2 were waited for; matrix products, arithmetic and copies ran while one was open for 9% of the time, Pallas kernels for 35%

profile of v3, /device:TPU:8, one launch (start us, length us, event | category | flops | bytes accessed | tf_op | source)
XLA Modules:
  0.0 453.8 jit_solution(17474193250160018021)
XLA Ops:
  7.2 0.0 copy-start
  7.2 0.0 copy-start.5
  7.2 0.0 all-gather.2.cloned.1.call-start
  7.2 0.7 all-gather.2.cloned.1.call-update
  7.9 0.9 compare_select_fusion
  8.8 0.3 copy-done
  9.1 2.4 gather_fusion
  11.5 0.0 copy-done.5
  11.5 3.9 fusion.7
  15.4 6.3 %all-to-all-start = ((bf16[3,16,8,1,4096]{4,2,0,3,1:T(8,128)(2,1)}), bf16[3,16,8,1,4096]{4,2,0,3,1:T(8,128)(2,1)S(1)}, u32[]{:S(2)}, u32[]{:S(2)}) async-start(bf16[3,16,8,1,4096]{4,2,0,3,1:T(8,128)(2,1)} %fusion.7), calls=%async_computation | async-start | bytes 6291456 | tf_op jit(solution)/shard_map/all_to_all | solution.py:142
  21.7 0.0 all-reduce.2.cloned.1.call-start
  21.7 4.5 copy.19
  26.3 99.5 %all-to-all-done = bf16[3,16,8,1,4096]{4,2,0,3,1:T(8,128)(2,1)S(1)} async-done(((bf16[3,16,8,1,4096]{4,2,0,3,1:T(8,128)(2,1)}), bf16[3,16,8,1,4096]{4,2,0,3,1:T(8,128)(2,1)S(1)}, u32[]{:S(2)}, u32[]{:S(2)}) %all-to-all-start) | async-done | bytes 3145760 | tf_op jit(solution)/shard_map/all_to_all | solution.py:142
  125.8 3.3 multiply_reduce_fusion.2
  129.1 0.1 copy.24
  129.2 0.1 copy.23
  129.3 0.1 reduce_sum.42
  129.3 5.1 %psum.21 = f32[3,128]{1,0:T(4,128)S(1)} all-reduce(f32[3,128]{1,0:T(4,128)S(1)} %reduce_sum.42), channel_id=1, replica_groups=mesh['section'=16,'tensor'=2] {'tensor'}, use_global_device_ids=true, to_apply=%region_1.2 | all-reduce | flops 384 | bytes 3072 | tf_op jit(solution)/shard_map/psum | solution.py:152
  134.5 0.0 copy-start.4
  134.5 4.5 copy_convert_fusion
  138.9 87.6 %all-gather.2.cloned.1.call-done = bf16[3584,4096]{1,0:T(8,128)(2,1)} async-done(((bf16[224,4096]{1,0:T(8,128)(2,1)}), bf16[3584,4096]{1,0:T(8,128)(2,1)}) %all-gather.2.cloned.1.call-update) | async-done | bytes 29360144 | tf_op jit(solution)/shard_map/all_gather | solution.py:144
  226.6 0.0 copy-done.4
  226.6 20.9 %fusion.3 = (bf16[384,4096]{1,0:T(8,128)(2,1)S(1)}, f32[4096]{0:T(1024)S(1)}, f32[4096,384]{0,1:T(8,128)}) fusion(f32[384]{0:T(512)S(1)} %get-tuple-element.11, f32[3,4096]{1,0:T(4,128)S(1)} %copy-done.4, f32[3,16,8,1,4096]{4,1,2,0,3:T(8,128)} %copy_convert_fusion, bf16[384,3584]{1,0:T(8,128)(2,1)} %bitcast.61, ...), kind=kOutput, calls=%fused_computation.6 | convolution fusion | flops 11285295104 | bytes 47908352 | tf_op jit(solution)/shard_map/dot_general | solution.py:148
  247.4 0.0 copy-start.3
  247.4 6.7 %multiply_reduce_fusion.1 = f32[3,4096]{1,0:T(4,128)S(1)} fusion(f32[3,128,4096]{2,1,0:T(8,128)} %bitcast.59, f32[3,128,4096]{2,1,0:T(8,128)} %bitcast.58, f32[3,128]{1,0:T(4,128)S(1)} %get-tuple-element.10, f32[3,4096]{1,0:T(4,128)S(1)} %copy-done.4), kind=kLoop, calls=%fused_computation.8 | loop fusion | flops 7852032 | bytes 12682752 | tf_op jit(solution)/shard_map/reduce_sum | solution.py:167
  254.2 0.7 pad_maximum_fusion
  254.8 0.0 all-reduce.2.cloned.1.call-update
  254.9 0.3 reduce-scatter.2.cloned.1.call-start
  255.1 0.0 copy-done.3
  255.1 17.2 %fusion.4 = bf16[3,128,3584]{2,1,0:T(8,128)(2,1)} fusion(bf16[3,128,4096]{2,1,0:T(8,128)(2,1)S(1)} %bitcast.62, bf16[3584,4096]{1,0:T(8,128)(2,1)} %all-gather.2.cloned.1.call-done), kind=kOutput, calls=%fused_computation.10 | convolution fusion | flops 11275665408 | bytes 35258368 | tf_op jit(solution)/shard_map/dot_general | solution.py:157
  272.3 0.0 reduce-scatter.2.cloned.1.call-update
  272.3 159.5 %reduce_terms.1 = f32[224,4096]{1,0:T(8,128)} custom-call(bf16[16,224,384]{2,1,0:T(8,128)(2,1)} %bitcast.63, bf16[384,4096]{1,0:T(8,128)(2,1)} %copy-done.3), custom_call_target="tpu_custom_call" | custom-call | flops 11274289152 | bytes 400000000 | tf_op jit(solution)/shard_map/reduce_terms/pallas_call | solution.py:109
  431.9 0.0 all-reduce.2.cloned.1.call-done
  431.9 1.5 slice_reduce_fusion
  433.4 5.5 %psum.23 = f32[]{:T(128)} all-reduce(f32[]{:T(128)} %slice_reduce_fusion), channel_id=1, replica_groups=mesh['section'=16,'tensor'=2] {'tensor'}, use_global_device_ids=true, to_apply=%region_6.7 | all-reduce | flops 1 | bytes 8 | tf_op jit(solution)/shard_map/psum | solution.py:171
  439.6 1.5 slice_multiply_fusion
  441.1 0.0 reduce-scatter.2.cloned.1.call-done
  441.1 0.0 copy-start.2
  441.1 0.0 copy-start.1
  441.1 3.2 convert_element_type.45
  444.3 0.0 copy-done.2
  444.3 1.8 copy.30
  446.1 0.0 copy-done.1
  (3 shorter events, 0.0 us)
Async XLA Ops:
  7.2 1.9 copy-start
  7.2 4.3 copy-start.5
  7.2 219.4 %all-gather.2.cloned.1.call-start = ((), (), s32[]{:S(2)}) async-start(), calls=%async_computation.2 | async-start | bytes 31195136 | tf_op jit(solution)/shard_map/all_gather | solution.py:144
  15.4 110.4 %all-to-all-start = ((bf16[3,16,8,1,4096]{4,2,0,3,1:T(8,128)(2,1)}), bf16[3,16,8,1,4096]{4,2,0,3,1:T(8,128)(2,1)S(1)}, u32[]{:S(2)}, u32[]{:S(2)}) async-start(bf16[3,16,8,1,4096]{4,2,0,3,1:T(8,128)(2,1)} %fusion.7), calls=%async_computation | async-start | bytes 6291456 | tf_op jit(solution)/shard_map/all_to_all | solution.py:142
  21.7 410.2 %all-reduce.2.cloned.1.call-start = ((), (), s32[]{:S(2)}) async-start(), calls=%async_computation.3 | async-start | bytes 131072 | tf_op jit(solution)/shard_map/psum | solution.py:169
  134.5 92.1 %copy-start.4 = (f32[3,4096]{1,0:T(4,128)S(1)}, f32[3,4096]{1,0:T(4,128)}, u32[]{:S(2)}) copy-start(f32[3,4096]{1,0:T(4,128)} %param.8) | copy-start | bytes 147460
  247.4 7.7 %copy-start.3 = (bf16[384,4096]{1,0:T(8,128)(2,1)}, bf16[384,4096]{1,0:T(8,128)(2,1)S(1)}, u32[]{:S(2)}) copy-start(bf16[384,4096]{1,0:T(8,128)(2,1)S(1)} %get-tuple-element.8.steer_ref) | copy-start | bytes 9437188
  254.9 186.2 %reduce-scatter.2.cloned.1.call-start = ((), (), s32[]{:S(2)}) async-start(), calls=%async_computation.4 | async-start | bytes 4128768 | tf_op jit(solution)/shard_map/reduce_scatter | solution.py:160
  441.1 3.2 copy-start.2
  441.1 5.1 %copy-start.1 = (bf16[3,128,4096]{2,1,0:T(8,128)(2,1)S(1)}, bf16[3,128,4096]{2,1,0:T(8,128)(2,1)}, u32[]{:S(2)}) copy-start(bf16[3,128,4096]{2,1,0:T(8,128)(2,1)} %param.5) | copy-start | bytes 9437188
Sparse Core Ops, SparseCore 0:
  9.6 216.9 all-gather.1
  255.0 87.1 all-reduce.1
  345.1 38.1 reduce-scatter.1

commit v4 on v1

--- a/solution.py
+++ b/solution.py
@@ -139,11 +139,12 @@
     rescale = float(total_rows) ** (-0.5)
     blocks = section_rows.reshape(3, sections, per_source, 1, width)
     outgoing = jnp.take(blocks, offsets, axis=1)
+    flat_student = student_rows.reshape(3 * seq_dev, student_width)
+    student_blocks = flat_student.T.reshape(sections, student_width // sections, 3 * seq_dev)
+    outgoing, student_blocks = lax.optimization_barrier((outgoing, student_blocks))
     incoming = lax.all_to_all(outgoing, "section", split_axis=1, concat_axis=3, tiled=True)
     target = incoming.reshape(3, seq_dev, width).astype(jnp.float32)
     whole_proj = lax.all_gather(proj, "section", axis=0, tiled=True)
-    flat_student = student_rows.reshape(3 * seq_dev, student_width)
-    student_blocks = flat_student.T.reshape(sections, student_width // sections, 3 * seq_dev)
     pred = jnp.dot(flat_student, whole_proj, preferred_element_type=jnp.float32).reshape(
         3, seq_dev, width
     )

time: 452 us -> 448 us (level)
  transfers between devices with their start and end apart: 3 -> 3, of which waited for: 1 -> 1; matrix products, arithmetic and copies ran while one was open for 8% -> 9% of each run, Pallas kernels for 35% -> 35%
where the time goes in v4:
time: 448 us
  Pallas kernels  159 us (35%)
  blocking collectives  121 us (27%)
  waiting for transfers between devices  86.9 us (19%)
  matrix products  39.4 us (9%)
  between operations  15.6 us (3%)
  local copies, waits for them, and re-layouts  15.4 us (3%)
  other arithmetic  10.6 us (2%)
    pallas_call x1, Pallas kernels, reduce_terms(): pl.pallas_call(functools.partial(reduce_kernel, n, rescale), out_shape=ja...  159 us
    all_to_all x1, blocking collectives, body(): lax.all_to_all(outgoing, 'section', split_axis=1, concat_axis=3, tiled=True)  110 us
    all_gather x1, waiting for transfers between devices, body(): whole_proj = lax.all_gather(proj, 'section', axis=0, tiled=True)  86.2 us
    dot_general x1, matrix products, body(): jnp.dot(flat_student, whole_proj, preferred_element_type=jnp.float32)  20.8 us
    dot_general x1, matrix products, body(): lax.dot_general(flat_steer, whole_proj, (((1,), (1,)), ((), ())), preferr...  18.6 us
  transfers between devices with their start and end apart: 3, of which 1 were waited for; matrix products, arithmetic and copies ran while one was open for 9% of the time, Pallas kernels for 35%

profile of v4, /device:TPU:8, one launch (start us, length us, event | category | flops | bytes accessed | tf_op | source)
XLA Modules:
  0.0 447.6 jit_solution(12531309777906040965)
XLA Ops:
  7.2 0.0 copy-start
  7.2 0.0 all-gather.2.cloned.1.call-start
  7.2 0.7 all-gather.2.cloned.1.call-update
  7.9 0.0 copy-start.4
  7.9 0.0 all-reduce.2.cloned.1.call-start
  8.0 4.7 %copy.16 = bf16[384,3584]{0,1:T(8,128)(2,1)} copy(bf16[384,3584]{1,0:T(8,128)(2,1)} %bitcast.36) | data formatting | bytes 5505024 | tf_op jit(solution)/shard_map/reshape | solution.py:142
  12.7 0.0 copy-done.4
  12.7 0.0 copy-done
  12.7 2.4 gather_fusion
  15.1 2.2 bitcast_select_fusion
  17.4 110.2 %all_to_all.4 = bf16[3,16,8,1,4096]{4,2,0,3,1:T(8,128)(2,1)S(1)} all-to-all(bf16[3,16,8,1,4096]{4,2,0,3,1:T(8,128)(2,1)S(1)} %bitcast.34), channel_id=1, replica_groups=mesh['section'=16,'tensor'=2] {'section'}, dimensions={1} | all-to-all | bytes 6291456 | tf_op jit(solution)/shard_map/all_to_all | solution.py:145
  127.5 0.8 convert_bitcast_fusion
  128.3 6.3 %copy.18 = f32[3,1,8,16,1,4096]{5,3,2,0,4,1:T(8,128)} copy(f32[3,1,8,16,1,4096]{5,2,0,3,4,1:T(8,128)S(1)} %convert_bitcast_fusion) | data formatting | bytes 12582912 | tf_op jit(solution)/shard_map/convert_element_type | solution.py:146
  134.6 0.0 copy-start.3
  134.6 0.7 fusion.5
  135.3 0.1 copy.20
  135.4 0.1 reduce_sum.42
  135.4 4.9 %psum.21 = f32[3,128]{1,0:T(4,128)S(1)} all-reduce(f32[3,128]{1,0:T(4,128)S(1)} %reduce_sum.42), channel_id=1, replica_groups=mesh['section'=16,'tensor'=2] {'tensor'}, use_global_device_ids=true, to_apply=%region_1.2 | all-reduce | flops 384 | bytes 3072 | tf_op jit(solution)/shard_map/psum | solution.py:152
  140.4 86.2 %all-gather.2.cloned.1.call-done = bf16[3584,4096]{1,0:T(8,128)(2,1)} async-done(((bf16[224,4096]{1,0:T(8,128)(2,1)}), bf16[3584,4096]{1,0:T(8,128)(2,1)}) %all-gather.2.cloned.1.call-update) | async-done | bytes 29360144 | tf_op jit(solution)/shard_map/all_gather | solution.py:147
  226.6 0.0 copy-done.3
  226.6 20.8 %multiply_reduce_fusion.1 = (f32[3,4096]{1,0:T(4,128)S(1)}, f32[4096]{0:T(1024)S(1)}, bf16[3,128,4096]{2,1,0:T(8,128)(2,1)}) fusion(f32[3,128]{1,0:T(4,128)S(1)} %multiply_add_fusion, f32[3,128,4096]{2,1,0:T(8,128)} %bitcast.35, f32[3,4096]{1,0:T(4,128)S(1)} %copy-done.3, bf16[3,128,3584]{2,1,0:T(8,128)(2,1)} %param.6, ...), kind=kOutput, calls=%fused_computation.11 | convolution fusion | flops 11288428544 | bytes 41666048 | tf_op jit(solution)/shard_map/dot_general | solution.py:148
  247.4 0.7 pad_maximum_fusion
  248.1 0.0 all-reduce.2.cloned.1.call-update
  248.1 0.2 reduce-scatter.2.cloned.1.call-start
  248.3 18.6 %fusion.6 = bf16[3,128,3584]{2,1,0:T(8,128)(2,1)} fusion(bf16[3,128,4096]{2,1,0:T(8,128)(2,1)} %get-tuple-element.10, bf16[3584,4096]{1,0:T(8,128)(2,1)} %all-gather.2.cloned.1.call-done), kind=kOutput, calls=%fused_computation.13 | convolution fusion | flops 11275665408 | bytes 35258368 | tf_op jit(solution)/shard_map/dot_general | solution.py:157
  266.9 0.0 reduce-scatter.2.cloned.1.call-update
  266.9 158.7 %reduce_terms.1 = f32[224,4096]{1,0:T(8,128)} custom-call(bf16[16,224,384]{2,1,0:T(8,128)(2,1)} %bitcast.37, bf16[384,4096]{1,0:T(8,128)(2,1)} %bitcast.40), custom_call_target="tpu_custom_call" | custom-call | flops 11274289152 | bytes 400000000 | tf_op jit(solution)/shard_map/reduce_terms/pallas_call | solution.py:109
  425.6 0.0 all-reduce.2.cloned.1.call-done
  425.6 1.5 slice_reduce_fusion
  427.1 5.5 %psum.23 = f32[]{:T(128)} all-reduce(f32[]{:T(128)} %slice_reduce_fusion), channel_id=1, replica_groups=mesh['section'=16,'tensor'=2] {'tensor'}, use_global_device_ids=true, to_apply=%region_6.7 | all-reduce | flops 1 | bytes 8 | tf_op jit(solution)/shard_map/psum | solution.py:171
  433.3 1.5 slice_multiply_fusion
  434.8 0.0 reduce-scatter.2.cloned.1.call-done
  434.8 0.0 copy-start.2
  434.8 0.0 copy-start.1
  434.8 3.2 convert_element_type.33
  438.1 0.0 copy-done.2
  438.1 1.8 copy.23
  439.9 0.0 copy-done.1
  (4 shorter events, 0.0 us)
Async XLA Ops:
  7.2 5.5 %copy-start = (bf16[3,128,4096]{2,1,0:T(8,128)(2,1)S(1)}, bf16[3,128,4096]{2,1,0:T(8,128)(2,1)}, u32[]{:S(2)}) copy-start(bf16[3,128,4096]{2,1,0:T(8,128)(2,1)} %param.5) | copy-start | bytes 9437188
  7.2 219.4 %all-gather.2.cloned.1.call-start = ((), (), s32[]{:S(2)}) async-start(), calls=%async_computation.2 | async-start | bytes 31195136 | tf_op jit(solution)/shard_map/all_gather | solution.py:147
  7.9 4.7 %copy-start.4 = (s32[16]{0:T(128)S(1)}, s32[16]{0:T(128)}, u32[]{:S(2)}) copy-start(s32[16]{0:T(128)} %param.9) | copy-start | bytes 196
  7.9 417.7 %all-reduce.2.cloned.1.call-start = ((), (), s32[]{:S(2)}) async-start(), calls=%async_computation.3 | async-start | bytes 131072 | tf_op jit(solution)/shard_map/psum | solution.py:169
  134.6 92.0 %copy-start.3 = (f32[3,4096]{1,0:T(4,128)S(1)}, f32[3,4096]{1,0:T(4,128)}, u32[]{:S(2)}) copy-start(f32[3,4096]{1,0:T(4,128)} %param.8) | copy-start | bytes 147460
  248.1 186.7 %reduce-scatter.2.cloned.1.call-start = ((), (), s32[]{:S(2)}) async-start(), calls=%async_computation.4 | async-start | bytes 4128768 | tf_op jit(solution)/shard_map/reduce_scatter | solution.py:160
  434.8 3.2 copy-start.2
  434.8 5.1 %copy-start.1 = (bf16[3,128,4096]{2,1,0:T(8,128)(2,1)S(1)}, bf16[3,128,4096]{2,1,0:T(8,128)(2,1)}, u32[]{:S(2)}) copy-start(bf16[3,128,4096]{2,1,0:T(8,128)(2,1)} %param.5) | copy-start | bytes 9437188
Sparse Core Ops, SparseCore 0:
  9.6 216.9 all-gather.1
  248.2 87.0 all-reduce.1
  338.3 38.0 reduce-scatter.1
